TPU v7x, 32 devices: a whole 2x2x4 slice. The times are simulated.
32 devices in a mesh: node: 8 (over z, x), feat: 4 (over y, core).
Axes of the slice: x: 2, y: 2, z: 4, core: 2. Of those that a mesh axis runs over, the one named last changes fastest.
Arguments:
- features: bfloat16 [768, 65536], P('feat', 'node'), may hold values from -6 to 6
- neighbors: int32 [4096, 25], P('node'), may hold values from 0 to 511
- degrees: int32 [4096], P('node'), may hold values from 1 to 25
- tile_src: int32 [32, 4], P('node'), may hold values from 0 to 63
- tile_count: int32 [32], P('node'), may hold values from 1 to 4
- w_self: bfloat16 [768, 1024], P('feat'), may hold values from -0.21875 to 0.21875
- w_neigh: bfloat16 [768, 1024], P('feat'), may hold values from -0.21875 to 0.21875
- out_bias: float32 [1024], replicated, may hold values from -3 to 3
- d_out: bfloat16 [4096, 1024], P(('node', 'feat')), may hold values from -6 to 6
Outputs:
- output: bfloat16 [4096, 1024], P(('node', 'feat'))
- grad_features: bfloat16 [768, 65536], P('feat', 'node')
- grad_neigh: float32 [768, 1024], P('feat', 'node')
All inputs are finite; a program needn't handle non-finite values.
Results may differ from a plain program's by a relative error of at most 0.0054.
Values may be sent and summed in bfloat16 or wider, within the bound.
A program may use at most 128 MiB of HBM per device.

v0:
```python
import math

import jax
import jax.numpy as jnp
from jax import lax
from jax.sharding import PartitionSpec as P

BLOCK = 128
KT = 4


def tile_counts(neighbors, degrees, tile_count, blocks, block, slot_count):
    fan_width = neighbors.shape[1]
    position = jnp.arange(fan_width, dtype=jnp.int32)
    block_live = jnp.repeat(tile_count, block)
    live_mask = (position[None, :] < degrees[:, None]) & (neighbors // block < block_live[:, None])
    slot_ids = jnp.arange(slot_count, dtype=jnp.int32)
    matches = (neighbors[:, :, None] == slot_ids[None, None, :]) & live_mask[:, :, None]
    tallies = jnp.sum(matches.astype(jnp.int32), axis=1)
    return tallies.astype(jnp.bfloat16).reshape(blocks, block, slot_count)


def dot_rows(left_cols, weights):
    return lax.dot_general(
        left_cols, weights, (((0,), (0,)), ((), ())), preferred_element_type=jnp.float32
    )


def dot_cols(weights, grad_pre):
    return lax.dot_general(
        weights, grad_pre, (((1,), (1,)), ((), ())), preferred_element_type=jnp.float32
    )


def body(features, neighbors, degrees, tile_src, tile_count, w_self, w_neigh, out_bias, d_out):
    feat_rows, src_width = features.shape
    node_count = neighbors.shape[0]
    blocks = tile_src.shape[0]
    slot_count = KT * BLOCK
    counts = tile_counts(neighbors, degrees, tile_count, blocks, BLOCK, slot_count)
    picked = features.reshape(feat_rows, src_width // BLOCK, BLOCK)[:, tile_src, :].reshape(
        feat_rows, blocks, slot_count
    )
    summed = jnp.einsum("dbk,bjk->dbj", picked, counts, preferred_element_type=jnp.float32)
    inverse = 1.0 / degrees.astype(jnp.float32)
    aggregate = (summed.reshape(feat_rows, node_count) * inverse).astype(jnp.bfloat16)
    own_cols = features[:, :node_count]
    aggregate_rows, own_rows = (
        lax.all_to_all(aggregate, "feat", split_axis=1, concat_axis=0, tiled=True),
        lax.all_to_all(own_cols, "feat", split_axis=1, concat_axis=0, tiled=True),
    )
    full_self, full_neigh = (
        lax.all_gather(w_self, "feat", axis=0, tiled=True),
        lax.all_gather(w_neigh, "feat", axis=0, tiled=True),
    )
    pre_act = dot_rows(own_rows, full_self) + dot_rows(aggregate_rows, full_neigh) + out_bias
    output = jax.nn.gelu(pre_act).astype(jnp.bfloat16)
    grad_pre = jax.vjp(jax.nn.gelu, pre_act)[1](d_out.astype(jnp.float32))[0].astype(jnp.bfloat16)
    grad_scale = 1.0 / math.sqrt(node_count * lax.axis_size("node"))
    partial_value = (
        jnp.dot(aggregate_rows, grad_pre, preferred_element_type=jnp.float32) * grad_scale
    )
    back_neigh = dot_cols(full_neigh, grad_pre).astype(jnp.bfloat16)
    back_self = dot_cols(full_self, grad_pre).astype(jnp.bfloat16)
    reduced = lax.psum_scatter(partial_value, "feat", scatter_dimension=0, tiled=True)
    grad_neigh = lax.psum_scatter(reduced, "node", scatter_dimension=1, tiled=True)
    neigh_cols, self_cols = (
        lax.all_to_all(back_neigh, "feat", split_axis=0, concat_axis=1, tiled=True),
        lax.all_to_all(back_self, "feat", split_axis=0, concat_axis=1, tiled=True),
    )
    scaled = (
        (neigh_cols.astype(jnp.float32) * inverse)
        .astype(jnp.bfloat16)
        .reshape(feat_rows, blocks, BLOCK)
    )
    spread = jnp.einsum("dbj,bjk->dbk", scaled, counts, preferred_element_type=jnp.float32)
    by_block = spread.reshape(feat_rows, blocks * KT, BLOCK).transpose(1, 0, 2)
    pooled = jax.ops.segment_sum(by_block, tile_src.reshape(-1), num_segments=src_width // BLOCK)
    grad_cols = pooled.transpose(1, 0, 2).reshape(feat_rows, src_width)
    grad_cols = grad_cols.at[:, :node_count].add(self_cols.astype(jnp.float32)).astype(jnp.bfloat16)
    return (output, grad_cols, grad_neigh)


def solution(mesh):
    placed = (
        P("feat", "node"),
        P("node", None),
        P("node"),
        P("node", None),
        P("node"),
        P("feat", None),
        P("feat", None),
        P(),
        P(("node", "feat"), None),
    )
    return jax.shard_map(
        body,
        mesh=mesh,
        in_specs=placed,
        out_specs=(P(("node", "feat"), None), P("feat", "node"), P("feat", "node")),
        check_vma=False,
    )
```

profile of v0, /device:TPU:0, one launch (start us, length us, event | category | flops | bytes accessed | tf_op | source)
XLA Modules:
  0.0 171.3 jit_solution(1067671729869136185)
XLA Ops:
  7.2 0.0 copy-start
  7.2 0.0 all-gather.3.cloned.1.call-start
  7.2 0.7 all-gather.3.cloned.1.call-update
  7.9 1.6 copy_bitcast_fusion.2
  9.6 4.2 %all-to-all-start = ((bf16[192,4,128]{2,0,1:T(8,128)(2,1)}), bf16[192,4,128]{2,0,1:T(8,128)(2,1)S(1)}, u32[]{:S(2)}, u32[]{:S(2)}) async-start(bf16[192,4,128]{2,0,1:T(8,128)(2,1)} %copy_bitcast_fusion.2), calls=%async_computation | async-start | bytes 393216 | tf_op jit(solution)/shard_map/all_to_all | solution.py:50
  13.8 0.7 all-gather.5.cloned.1.call-update
  14.5 0.7 compare_select_fusion
  15.2 0.1 reshape.85
  15.3 0.1 broadcast_bitcast_fusion
  15.4 0.9 fusion.24
  16.3 5.9 %convert_reduce_fusion = s32[512,512]{1,0:T(8,128)S(1)} fusion(s32[512,25]{0,1:T(8,128)} %param.12, pred[512,25]{0,1:T(8,128)(4,1)S(1)} %fusion.24), kind=kLoop, calls=%fused_computation.2 | loop fusion | flops 25952256 | bytes 1112576 | tf_op jit(solution)/shard_map/reduce_sum | solution.py:19
  22.2 0.9 convert_element_type.66
  23.1 2.8 %copy_bitcast_fusion.1 = bf16[192,64,128]{2,0,1:T(8,128)(2,1)S(1)} fusion(bf16[192,8192]{1,0:T(8,128)(2,1)} %param.11), kind=kLoop, calls=%fused_computation.6 | loop fusion | bytes 6291456 | tf_op jit(solution)/shard_map/reshape | solution.py:41
  25.9 0.0 copy-start.6
  26.0 1.5 gather_fusion
  27.5 2.4 %fusion.5 = bf16[192,4,128]{2,0,1:T(8,128)(2,1)} fusion(bf16[4,128,512]{2,1,0:T(8,128)(2,1)} %bitcast.67, bf16[4,4,24,8,128]{4,3,2,1,0:T(8,128)(2,1)} %bitcast.72, f32[4,128]{1,0:T(4,128)S(1)} %divide_bitcast_fusion), kind=kOutput, calls=%fused_computation.17 | convolution fusion | flops 100859904 | bytes 1509376 | tf_op jit(solution)/shard_map/dbk,bjk->dbj/dot_general | solution.py:44
  29.9 3.4 %all-to-all-start.1 = ((bf16[192,4,128]{2,0,1:T(8,128)(2,1)}), bf16[192,4,128]{2,0,1:T(8,128)(2,1)S(1)}, u32[]{:S(2)}, u32[]{:S(2)}) async-start(bf16[192,4,128]{2,0,1:T(8,128)(2,1)} %fusion.5), calls=%async_computation.1 | async-start | bytes 393216 | tf_op jit(solution)/shard_map/all_to_all | solution.py:49
  33.3 0.0 reduce-scatter.3.cloned.1.call-start
  33.3 0.0 all-gather.3.cloned.1.call-done
  33.3 1.8 %fusion.26 = f32[128,1024]{1,0:T(8,128)S(1)} fusion(bf16[768,128]{1,0:T(8,128)(2,1)S(1)} %bitcast.71, bf16[768,1024]{1,0:T(8,128)(2,1)} %all-gather.3.cloned.1.call-done), kind=kOutput, calls=%fused_computation.58 | convolution fusion | flops 201326592 | bytes 2293760 | tf_op jit(solution)/shard_map/dot_general | solution.py:24
  35.2 3.4 %all-to-all-done.1 = bf16[192,4,128]{2,0,1:T(8,128)(2,1)S(1)} async-done(((bf16[192,4,128]{2,0,1:T(8,128)(2,1)}), bf16[192,4,128]{2,0,1:T(8,128)(2,1)S(1)}, u32[]{:S(2)}, u32[]{:S(2)}) %all-to-all-start.1) | async-done | bytes 196640 | tf_op jit(solution)/shard_map/all_to_all | solution.py:49
  38.6 14.6 %all-gather.5.cloned.1.call-done = bf16[768,1024]{1,0:T(8,128)(2,1)} async-done(((bf16[192,1024]{1,0:T(8,128)(2,1)}), bf16[768,1024]{1,0:T(8,128)(2,1)}) %all-gather.5.cloned.1.call-update) | async-done | bytes 1572880 | tf_op jit(solution)/shard_map/all_gather | solution.py:54
  53.2 2.9 %fusion.10 = (bf16[128,1024]{1,0:T(8,128)(2,1)S(1)}, bf16[128,1024]{1,0:T(8,128)(2,1)}) fusion(bf16[128,1024]{1,0:T(8,128)(2,1)S(1)} %copy-done.5, f32[1024]{0:T(1024)S(1)} %copy-done.6, f32[128,1024]{1,0:T(8,128)S(1)} %fusion.26, bf16[768,128]{1,0:T(8,128)(2,1)S(1)} %bitcast.69, bf16[768,1024]{1,0:T(8,128)(2,1)} %all-gather.5.cloned.1.call-done), kind=kOutput, calls=%fused_computation.27 | convolution fusion | flops 204603392 | bytes 3084288 | tf_op jit(solution)/shard_map/dot_general | solution.py:24
  56.1 2.2 %convolution_multiply_fusion = f32[768,1024]{1,0:T(8,128)} fusion(bf16[768,128]{1,0:T(8,128)(2,1)S(1)} %bitcast.70, bf16[128,1024]{1,0:T(8,128)(2,1)S(1)} %get-tuple-element.15), kind=kOutput, calls=%fused_computation.7 | convolution fusion | flops 202113024 | bytes 3604480 | tf_op jit(solution)/shard_map/dot_general | solution.py:61
  58.3 0.0 reduce-scatter.3.cloned.1.call-update
  58.4 0.1 reshape.93
  58.5 0.7 compare_reduce_fusion
  59.2 2.1 %fusion.3 = bf16[768,128]{0,1:T(8,128)(2,1)S(1)} fusion(bf16[128,1024]{1,0:T(8,128)(2,1)S(1)} %get-tuple-element.15, bf16[768,1024]{1,0:T(8,128)(2,1)} %all-gather.5.cloned.1.call-done), kind=kOutput, calls=%fused_computation.15 | convolution fusion | flops 201424896 | bytes 2031616 | tf_op jit(solution)/shard_map/dot_general | solution.py:30
  61.3 0.8 copy.51
  62.1 3.4 %all-to-all-start.2 = ((bf16[4,192,128]{2,1,0:T(8,128)(2,1)}), bf16[4,192,128]{2,1,0:T(8,128)(2,1)S(1)}, u32[]{:S(2)}, u32[]{:S(2)}) async-start(bf16[4,192,128]{2,1,0:T(8,128)(2,1)} %bitcast.11), calls=%async_computation.2 | async-start | bytes 393216 | tf_op jit(solution)/shard_map/all_to_all | solution.py:68
  65.5 0.7 fusion.4
  66.1 0.8 copy.55
  66.9 3.8 %all-to-all-done.2 = bf16[4,192,128]{2,1,0:T(8,128)(2,1)S(1)} async-done(((bf16[4,192,128]{2,1,0:T(8,128)(2,1)}), bf16[4,192,128]{2,1,0:T(8,128)(2,1)S(1)}, u32[]{:S(2)}, u32[]{:S(2)}) %all-to-all-start.2) | async-done | bytes 196640 | tf_op jit(solution)/shard_map/all_to_all | solution.py:68
  70.7 3.4 %all-to-all-start.3 = ((bf16[4,192,128]{2,1,0:T(8,128)(2,1)}), bf16[4,192,128]{2,1,0:T(8,128)(2,1)S(1)}, u32[]{:S(2)}, u32[]{:S(2)}) async-start(bf16[4,192,128]{2,1,0:T(8,128)(2,1)} %bitcast.17), calls=%async_computation.3 | async-start | bytes 393216 | tf_op jit(solution)/shard_map/all_to_all | solution.py:69
  74.1 0.0 reduce-scatter.5.cloned.1.call-start
  74.2 0.3 convolution_bitcast_fusion
  74.5 1.0 copy.52
  75.5 0.6 reshape.80
  76.2 0.5 copy.53
  76.7 3.4 %broadcast_in_dim.8 = f32[64,192,128]{2,1,0:T(8,128)} broadcast(f32[]{:T(128)} %constant.60.clone.1), dimensions={} | broadcast | bytes 6291460 | tf_op jit(solution)/shard_map/broadcast_in_dim | solution.py:78
  80.1 4.0 %scatter_fusion = f32[64,192,128]{2,1,0:T(8,128)} fusion(f32[64,192,128]{2,1,0:T(8,128)} %broadcast_in_dim.8, s32[16]{0:T(128)S(1)} %reshape.93, f32[16,192,128]{2,1,0:T(8,128)S(1)} %copy.53), kind=kCustom, calls=%fused_computation.1 | custom fusion | flops 393216 | bytes 4718656 | tf_op jit(solution)/shard_map/scatter-add | solution.py:78
  84.1 13.4 %reduce-scatter.3.cloned.1.call-done = f32[192,1024]{1,0:T(8,128)} async-done(((f32[768,1024]{1,0:T(8,128)}), f32[192,1024]{1,0:T(8,128)}) %reduce-scatter.3.cloned.1.call-update) | async-done | bytes 786448 | tf_op jit(solution)/shard_map/reduce_scatter | solution.py:65
  97.5 0.0 reduce-scatter.5.cloned.1.call-update
  97.5 6.2 %copy_bitcast_fusion = f32[192,8192]{1,0:T(8,128)} fusion(f32[64,192,128]{2,1,0:T(8,128)} %scatter_fusion), kind=kLoop, calls=%fused_computation.5 | loop fusion | bytes 12582912 | tf_op jit(solution)/shard_map/reshape | solution.py:79
  103.7 0.0 all-to-all-done.3
  103.7 2.5 %fusion.18 = f32[192,8192]{1,0:T(8,128)} fusion(f32[192,8192]{1,0:T(8,128)} %copy_bitcast_fusion, pred[]{:T(512)} %compare_reduce_fusion, bf16[4,192,128]{2,1,0:T(8,128)(2,1)S(1)} %all-to-all-done.3), kind=kLoop, calls=%fused_computation.36 | loop fusion | flops 294912 | bytes 983552 | tf_op jit(solution)/shard_map/scatter-add | solution.py:80
  106.2 4.9 %convert_element_type.84 = bf16[192,8192]{1,0:T(8,128)(2,1)} convert(f32[192,8192]{1,0:T(8,128)} %fusion.18) | non-fusion elementwise | flops 1572864 | bytes 9437184 | tf_op jit(solution)/shard_map/convert_element_type | solution.py:80
  111.1 53.6 %reduce-scatter.5.cloned.1.call-done = f32[192,128]{1,0:T(8,128)} async-done(((f32[192,1024]{1,0:T(8,128)}), f32[192,128]{1,0:T(8,128)}) %reduce-scatter.5.cloned.1.call-update) | async-done | bytes 98320 | tf_op jit(solution)/shard_map/reduce_scatter | solution.py:66
  (16 shorter events, 0.0 us)
Async XLA Ops:
  7.2 8.1 %copy-start = (s32[4]{0:T(128)S(1)}, s32[4]{0:T(128)}, u32[]{:S(2)}) copy-start(s32[4]{0:T(128)} %param.15) | copy-start | bytes 52
  7.2 26.1 %all-gather.3.cloned.1.call-start = ((), (), s32[]{:S(2)}) async-start(), calls=%async_computation.6 | async-start | bytes 1966080 | tf_op jit(solution)/shard_map/all_gather | solution.py:53
  9.6 20.3 %all-to-all-start = ((bf16[192,4,128]{2,0,1:T(8,128)(2,1)}), bf16[192,4,128]{2,0,1:T(8,128)(2,1)S(1)}, u32[]{:S(2)}, u32[]{:S(2)}) async-start(bf16[192,4,128]{2,0,1:T(8,128)(2,1)} %copy_bitcast_fusion.2), calls=%async_computation | async-start | bytes 393216 | tf_op jit(solution)/shard_map/all_to_all | solution.py:50
  13.8 39.4 %all-gather.5.cloned.1.call-start = ((), (), s32[]{:S(2)}) async-start(), calls=%async_computation.7 | async-start | bytes 1966080 | tf_op jit(solution)/shard_map/all_gather | solution.py:54
  23.1 4.3 %copy-start.3 = (s32[512]{0:T(512)S(1)}, s32[512]{0:T(512)}, u32[]{:S(2)}) copy-start(s32[512]{0:T(512)} %param.13) | copy-start | bytes 6148
  25.9 27.3 %copy-start.6 = (f32[1024]{0:T(1024)S(1)}, f32[1024]{0:T(1024)}, u32[]{:S(2)}) copy-start(f32[1024]{0:T(1024)} %param.18) | copy-start | bytes 12292
  27.5 25.7 %copy-start.5 = (bf16[128,1024]{1,0:T(8,128)(2,1)S(1)}, bf16[128,1024]{1,0:T(8,128)(2,1)}, u32[]{:S(2)}) copy-start(bf16[128,1024]{1,0:T(8,128)(2,1)} %param.19) | copy-start | bytes 786436
  29.9 8.7 %all-to-all-start.1 = ((bf16[192,4,128]{2,0,1:T(8,128)(2,1)}), bf16[192,4,128]{2,0,1:T(8,128)(2,1)S(1)}, u32[]{:S(2)}, u32[]{:S(2)}) async-start(bf16[192,4,128]{2,0,1:T(8,128)(2,1)} %fusion.5), calls=%async_computation.1 | async-start | bytes 393216 | tf_op jit(solution)/shard_map/all_to_all | solution.py:49
  33.3 64.3 %reduce-scatter.3.cloned.1.call-start = ((), (), s32[]{:S(2)}) async-start(), calls=%async_computation.8 | async-start | bytes 3932160 | tf_op jit(solution)/shard_map/reduce_scatter | solution.py:65
  56.1 2.3 %copy-start.4 = (s32[4,4]{1,0:T(4,128)S(1)}, s32[4,4]{1,0:T(4,128)}, u32[]{:S(2)}) copy-start(s32[4,4]{1,0:T(4,128)} %param.14) | copy-start | bytes 196
  58.3 7.1 %copy-start.1 = (bf16[768,1024]{1,0:T(8,128)(2,1)S(1)}, bf16[768,1024]{1,0:T(8,128)(2,1)}, u32[]{:S(2)}) copy-start(bf16[768,1024]{1,0:T(8,128)(2,1)} %all-gather.3.cloned.1.call-done) | copy-start | bytes 4718596
  58.4 15.8 %copy-start.2 = (bf16[512,512]{1,0:T(8,128)(2,1)S(1)}, bf16[512,512]{1,0:T(8,128)(2,1)}, u32[]{:S(2)}) copy-start(bf16[512,512]{1,0:T(8,128)(2,1)} %convert_element_type.66) | copy-start | bytes 1572868
  62.1 8.7 %all-to-all-start.2 = ((bf16[4,192,128]{2,1,0:T(8,128)(2,1)}), bf16[4,192,128]{2,1,0:T(8,128)(2,1)S(1)}, u32[]{:S(2)}, u32[]{:S(2)}) async-start(bf16[4,192,128]{2,1,0:T(8,128)(2,1)} %bitcast.11), calls=%async_computation.2 | async-start | bytes 393216 | tf_op jit(solution)/shard_map/all_to_all | solution.py:68
  70.7 33.0 %all-to-all-start.3 = ((bf16[4,192,128]{2,1,0:T(8,128)(2,1)}), bf16[4,192,128]{2,1,0:T(8,128)(2,1)S(1)}, u32[]{:S(2)}, u32[]{:S(2)}) async-start(bf16[4,192,128]{2,1,0:T(8,128)(2,1)} %bitcast.17), calls=%async_computation.3 | async-start | bytes 393216 | tf_op jit(solution)/shard_map/all_to_all | solution.py:69
  74.1 90.6 %reduce-scatter.5.cloned.1.call-start = ((), (), s32[]{:S(2)}) async-start(), calls=%async_computation.9 | async-start | bytes 884736 | tf_op jit(solution)/shard_map/reduce_scatter | solution.py:66
Sparse Core Ops, SparseCore 0:
  9.6 22.3 all-gather.2
  33.5 19.6 all-gather.4
  58.5 38.9 reduce-scatter.2
  101.6 63.0 reduce-scatter.4
where the time goes:
time: 172 us; the launch traced here: 171 us
  waiting for transfers between devices  90.4 us (53%)
  other arithmetic  20.6 us (12%)
  local copies, waits for them, and re-layouts  19.6 us (11%)
  starting transfers between devices  14.5 us (8%)
  between operations  13.9 us (8%)
  matrix products  12.4 us (7%)
    reduce_scatter x1, waiting for transfers between devices, body(): lax.psum_scatter(reduced, 'node', scatter_dimension=1, tiled=True)  53.6 us
    all_gather x1, waiting for transfers between devices, body(): lax.all_gather(w_neigh, 'feat', axis=0, tiled=True)  14.6 us
    reduce_scatter x1, waiting for transfers between devices, body(): lax.psum_scatter(partial_value, 'feat', scatter_dimension=0, tiled=True)  13.4 us
    reshape x1, local copies, waits for them, and re-layouts, body(): grad_cols = pooled.transpose(1, 0, 2).reshape(feat_rows, src_width)  6.16 us
    reduce_sum x1, other arithmetic, tile_counts(): tallies = jnp.sum(matches.astype(jnp.int32), axis=1)  5.91 us
    convert_element_type x1, other arithmetic, body(): grad_cols.at[:, :node_count].add(self_cols.astype(jnp.float32))  4.9 us
    dot_general x2, matrix products, dot_rows(): lax.dot_general(left_cols, weights, (((0,), (0,)), ((), ())), preferred_e...  4.71 us
    all_to_all x1, starting transfers between devices, body(): lax.all_to_all(own_cols, 'feat', split_axis=1, concat_axis=0, tiled=True)  4.24 us
  transfers between devices with their start and end apart: 8, of which 5 were waited for; matrix products, arithmetic and copies ran while one was open for 28% of the time, Pallas kernels for 0%

commit v1 on v0

--- a/solution.py
+++ b/solution.py
@@ -1,8 +1,11 @@
+import functools
 import math
 
 import jax
 import jax.numpy as jnp
 from jax import lax
+from jax.experimental import pallas as pl
+from jax.experimental.pallas import tpu as pltpu
 from jax.sharding import PartitionSpec as P
 
 BLOCK = 128
@@ -80,8 +83,346 @@
     grad_cols = grad_cols.at[:, :node_count].add(self_cols.astype(jnp.float32)).astype(jnp.bfloat16)
     return (output, grad_cols, grad_neigh)
 
+MESH = pl.DeviceIdType.MESH
+F32 = jnp.float32
+BF16 = jnp.bfloat16
+
+
+def remote(src, dst, send_sem, recv_sem, device):
+    return pltpu.make_async_remote_copy(
+        src_ref=src, dst_ref=dst, send_sem=send_sem, recv_sem=recv_sem, device_id=device, device_id_type=MESH
+    )
+
+
+def gather_kernel(tile_src, tile_count, features, nbrs, degrees, x_rows, x_trans, counts, own_cols, picked, own_sem, tile_sem):
+    rows = features.shape[0]
+    blocks = tile_src.shape[0]
+    own = blocks * BLOCK
+    fan = nbrs.shape[1]
+    own_copy = pltpu.make_async_copy(features.at[:, pl.ds(0, own)], own_cols, own_sem)
+    own_copy.start()
+    copies = []
+    for b in range(blocks):
+        for k in range(KT):
+            start = pl.multiple_of(tile_src[b, k] * BLOCK, BLOCK)
+            copies.append(
+                pltpu.make_async_copy(
+                    features.at[:, pl.ds(start, BLOCK)],
+                    picked.at[b, :, pl.ds(k * BLOCK, BLOCK)],
+                    tile_sem.at[b * KT + k],
+                )
+            )
+            copies[-1].start()
+
+    def count_tile(tile, carry):
+        b, k = tile // KT, tile % KT
+        nb = nbrs[b]
+        slot = lax.broadcasted_iota(jnp.int32, nb.shape, 0)
+        live = (slot < degrees[b]) & (nb < tile_count[b] * BLOCK)
+        offset = jnp.where(live, nb - k * BLOCK, -1)
+        ids = lax.broadcasted_iota(jnp.int32, (BLOCK, BLOCK), 0)
+        total = jnp.zeros((BLOCK, BLOCK), F32)
+        for j in range(fan):
+            total = total + jnp.where(ids == offset[j:j + 1, :], 1.0, 0.0)
+        counts[tile] = total.astype(BF16)
+        return carry
+
+    lax.fori_loop(0, blocks * KT, count_tile, 0)
+    own_copy.wait()
+    x_rows[pl.ds(0, rows), :] = own_cols[...]
+    for copy in copies:
+        copy.wait()
+    for b in range(blocks):
+        tally = counts[pl.ds(b * KT, KT)].reshape(KT * BLOCK, BLOCK)
+        summed = jnp.dot(picked[b], tally, preferred_element_type=F32)
+        inverse = 1.0 / degrees[b].astype(F32)
+        x_rows[pl.ds(rows, rows), pl.ds(b * BLOCK, BLOCK)] = (summed * inverse).astype(BF16)
+    x_trans[...] = x_rows[...].T
+
+
+def place_kernel(position, spread, back_self, grad_cols):
+    step = pl.program_id(0)
+    per = grad_cols.shape[1] // BLOCK
+    tiles = spread.shape[0]
+    own = back_self.shape[1] // BLOCK
+
+    def value(i):
+        at = position[step * per + i]
+        tile = spread[jnp.minimum(at, tiles - 1)]
+        return jnp.where(at < tiles, tile, 0.0)
+
+    @pl.when(step == 0)
+    def _():
+        for i in range(per):
+            tile = value(i)
+            if i < own:
+                tile = tile + back_self[:, i * BLOCK:(i + 1) * BLOCK].astype(F32)
+            grad_cols[:, i * BLOCK:(i + 1) * BLOCK] = tile.astype(BF16)
+
+    @pl.when(step > 0)
+    def _():
+        for i in range(per):
+            grad_cols[:, i * BLOCK:(i + 1) * BLOCK] = value(i).astype(BF16)
+
+
+def layer_kernel(
+    n_node, grad_scale,
+    same, x_rows, x_trans, counts, degrees, w_self, w_neigh, bias, d_out,
+    output, spread, back_self, grad_neigh,
+    merged, weights, partial_sum, core_in, y_out, y_in, grads, back, node_out, node_in,
+    core_send, core_recv, y_send, y_recv, gy_send, gy_recv, gc_send, gc_recv, fw_send, fw_recv,
+    node_send, node_recv,
+):
+    node = lax.axis_index("node")
+    feat = lax.axis_index("feat")
+    y, core = feat // 2, feat % 2
+    rows = w_self.shape[0]
+    blocks = degrees.shape[0]
+    tiles = blocks * KT
+    n_chunks = n_node // 2
+    hid = bias.shape[1]
+    width = hid // n_chunks
+    half = width // 2
+    core_feat = y * 2 + (1 - core)
+    y_feat = (1 - y) * 2 + core
+    diag_feat = (1 - y) * 2 + (1 - core)
+    core_dev = (node, core_feat)
+    y_dev = (node, y_feat)
+
+    barrier = pltpu.get_barrier_semaphore()
+    pl.semaphore_signal(barrier, inc=1, device_id=core_dev, device_id_type=MESH)
+    pl.semaphore_signal(barrier, inc=1, device_id=y_dev, device_id_type=MESH)
+    for step in range(1, n_node):
+        pl.semaphore_signal(barrier, inc=1, device_id=((node + step) % n_node, feat), device_id_type=MESH)
+
+    own = blocks * BLOCK
+    weights[pl.ds(0, rows), :] = w_self[...]
+    weights[pl.ds(rows, rows), :] = w_neigh[...]
+
+    pl.semaphore_wait(barrier, n_node + 1)
+
+    def columns(step):
+        chunk = (node // 2 + step + 1) % n_chunks
+        return chunk, pl.ds(pl.multiple_of(chunk * width, width), width)
+
+    def core_copy(step):
+        return remote(
+            partial_sum.at[step, :, 1 - core], core_in.at[step], core_send.at[step], core_recv.at[step], core_dev
+        )
+
+    def y_copy(step):
+        return remote(y_out.at[step], y_in.at[step], y_send.at[step], y_recv.at[step], y_dev)
+
+    def grad_y(step, slot):
+        ref = grads.at[step, slot]
+        return remote(ref, ref, gy_send.at[step], gy_recv.at[step], y_dev)
+
+    def grad_core(step, slot):
+        ref = grads.at[step, slot]
+        return remote(ref, ref, gc_send.at[step], gc_recv.at[step], core_dev)
+
+    def grad_forward(step, slot):
+        ref = grads.at[step, slot]
+        return remote(ref, ref, fw_send.at[step], fw_recv.at[step], core_dev)
+
+    def node_copy(step, side, target, sender):
+        return remote(
+            node_out.at[step, side], node_in.at[sender], node_send.at[step, side], node_recv.at[sender],
+            (target, feat),
+        )
+
+    def to_y(step):
+        core_copy(step).wait_recv()
+        y_out[step] = (partial_sum[step, 1 - y, core] + core_in[step, 1 - y]).astype(BF16)
+        y_copy(step).start()
+
+    for step in range(n_chunks):
+        _, cols = columns(step)
+        product = jnp.dot(x_trans[...], weights[:, cols], preferred_element_type=F32)
+        partial_sum[step] = product.reshape(2, 2, BLOCK, width)
+        core_copy(step).start()
+        if step >= 1:
+            to_y(step - 1)
+    to_y(n_chunks - 1)
+
+    def merge_tile(tile, carry):
+        for b in range(blocks):
+            total = jnp.zeros((BLOCK, BLOCK), F32)
+            for k in range(KT):
+                total = total + counts[b * KT + k].astype(F32) * same[tile, b * KT + k]
+            merged[tile, :, pl.ds(b * BLOCK, BLOCK)] = total.astype(BF16)
+        return carry
+
+    lax.fori_loop(0, tiles, merge_tile, 0)
+
+    def activate(step):
+        _, cols = columns(step)
+        y_copy(step).wait_recv()
+        v = partial_sum[step, y, core] + core_in[step, y] + y_in[step].astype(F32) + bias[:, cols]
+        root = math.sqrt(2.0 / math.pi)
+        square = v * v
+        bend = jnp.tanh(root * v * (1.0 + 0.044715 * square))
+        rise = 0.5 * (1.0 + bend)
+        output[:, cols] = (v * rise).astype(BF16)
+        slope = rise + 0.5 * v * (1.0 - bend * bend) * (root * (1.0 + 3.0 * 0.044715 * square))
+        grads[step, feat] = (d_out[:, cols].astype(F32) * slope).astype(BF16)
+        grad_y(step, feat).start()
+        grad_core(step, feat).start()
+
+    def forward(step):
+        grad_y(step, y_feat).wait_recv()
+        grad_forward(step, y_feat).start()
+
+    def backward(step):
+        chunk, cols = columns(step)
+        grad_core(step, core_feat).wait_recv()
+        grad_forward(step, diag_feat).wait_recv()
+        g = grads[step].reshape(blocks * BLOCK, width)
+        part = jnp.dot(x_rows[pl.ds(rows, rows), :], g, preferred_element_type=F32)
+        for side in range(2):
+            piece = part[:, side * half:(side + 1) * half]
+            node_out[step, side] = piece.astype(BF16)
+            if step < n_chunks - 1:
+                node_copy(step, side, chunk * 2 + side, node).start()
+        if step == n_chunks - 1:
+            other = 1 - node % 2
+            node_copy(step, other, chunk * 2 + other, node).start()
+            mine = (node % 2).astype(F32)
+            grad_neigh[...] = part[:, half:] * mine + part[:, :half] * (1.0 - mine)
+        term = lax.dot_general(weights[:, cols], g, (((1,), (1,)), ((), ())), preferred_element_type=F32)
+        if step == 0:
+            back[...] = term
+        else:
+            back[...] += term
+
+    for step in range(n_chunks + 2):
+        if step < n_chunks:
+            activate(step)
+        if 1 <= step <= n_chunks:
+            forward(step - 1)
+        if step >= 2:
+            backward(step - 2)
+
+    scaled = jnp.concatenate(
+        [
+            (
+                back[pl.ds(rows, rows), pl.ds(b * BLOCK, BLOCK)].astype(BF16).astype(F32)
+                * (1.0 / degrees[b].astype(F32))
+            ).astype(BF16)
+            for b in range(blocks)
+        ],
+        axis=1,
+    )
+    for pair in range(tiles // 2):
+        both = merged[pl.ds(pair * 2, 2)].reshape(2 * BLOCK, own)
+        result = lax.dot_general(scaled, both, (((1,), (1,)), ((), ())), preferred_element_type=F32)
+        spread[pair * 2] = result[:, :BLOCK]
+        spread[pair * 2 + 1] = result[:, BLOCK:]
+    back_self[...] = back[pl.ds(0, rows), :].astype(BF16)
+
+    total = grad_neigh[...]
+    for step in range(1, n_node):
+        sender = (node + step) % n_node
+        node_copy(0, 0, sender, sender).wait_recv()
+        total = total + node_in[sender].astype(F32)
+    grad_neigh[...] = total * grad_scale
+
+    for step in range(n_chunks):
+        core_copy(step).wait_send()
+        y_copy(step).wait_send()
+        grad_y(step, feat).wait_send()
+        grad_core(step, feat).wait_send()
+        grad_forward(step, y_feat).wait_send()
+        if step < n_chunks - 1:
+            for side in range(2):
+                node_copy(step, side, (node + 1) % n_node, node).wait_send()
+    other = 1 - node % 2
+    node_copy(n_chunks - 1, other, node - node % 2 + other, node).wait_send()
+
+
+def kernel_body(n_node, features, neighbors, degrees, tile_src, tile_count, w_self, w_neigh, out_bias, d_out):
+    rows, src_width = features.shape
+    nodes = neighbors.shape[0]
+    blocks = tile_src.shape[0]
+    tiles = blocks * KT
+    hid = out_bias.shape[0]
+    n_chunks = n_node // 2
+    width = hid // n_chunks
+    half = width // 2
+    src_blocks = src_width // BLOCK
+    flat = tile_src.reshape(-1)
+    match = flat[None, :] == jnp.arange(src_blocks, dtype=jnp.int32)[:, None]
+    found = jnp.max(jnp.where(match, jnp.arange(tiles, dtype=jnp.int32)[None, :], -1), axis=1)
+    position = jnp.where(found < 0, tiles, found)
+    nbrs = neighbors.reshape(blocks, BLOCK, -1).transpose(0, 2, 1)
+    same = (flat[:, None] == flat[None, :]).astype(F32)
+    degrees = degrees.reshape(blocks, 1, BLOCK)
+    smem = pl.BlockSpec(memory_space=pltpu.SMEM)
+    vmem = pl.BlockSpec(memory_space=pltpu.VMEM)
+    dma = pltpu.SemaphoreType.DMA
+    x_rows, x_trans, counts = pl.pallas_call(
+        gather_kernel,
+        out_shape=(
+            jax.ShapeDtypeStruct((2 * rows, nodes), BF16),
+            jax.ShapeDtypeStruct((nodes, 2 * rows), BF16),
+            jax.ShapeDtypeStruct((tiles, BLOCK, BLOCK), BF16),
+        ),
+        in_specs=[smem, smem, pl.BlockSpec(memory_space=pl.ANY), vmem, vmem],
+        out_specs=(vmem,) * 3,
+        scratch_shapes=[
+            pltpu.VMEM((rows, nodes), BF16),
+            pltpu.VMEM((blocks, rows, KT * BLOCK), BF16),
+            dma,
+            dma((tiles,)),
+        ],
+        compiler_params=pltpu.CompilerParams(vmem_limit_bytes=24 * 1024 * 1024),
+    )(tile_src, tile_count, features, nbrs, degrees)
+    output, spread, back_self, grad_neigh = pl.pallas_call(
+        functools.partial(layer_kernel, n_node, 1.0 / math.sqrt(nodes * n_node)),
+        out_shape=(
+            jax.ShapeDtypeStruct(d_out.shape, BF16),
+            jax.ShapeDtypeStruct((tiles, rows, BLOCK), F32),
+            jax.ShapeDtypeStruct((rows, nodes), BF16),
+            jax.ShapeDtypeStruct((rows, half), F32),
+        ),
+        in_specs=[smem] + [vmem] * 8,
+        out_specs=(vmem,) * 4,
+        scratch_shapes=[
+            pltpu.VMEM((tiles, BLOCK, nodes), BF16),
+            pltpu.VMEM((2 * rows, hid), BF16),
+            pltpu.VMEM((n_chunks, 2, 2, BLOCK, width), F32),
+            pltpu.VMEM((n_chunks, 2, BLOCK, width), F32),
+            pltpu.VMEM((n_chunks, BLOCK, width), BF16),
+            pltpu.VMEM((n_chunks, BLOCK, width), BF16),
+            pltpu.VMEM((n_chunks, 4, BLOCK, width), BF16),
+            pltpu.VMEM((2 * rows, nodes), F32),
+            pltpu.VMEM((n_chunks, 2, rows, half), BF16),
+            pltpu.VMEM((n_node, rows, half), BF16),
+        ]
+        + [dma((n_chunks,))] * 10
+        + [dma((n_chunks, 2)), dma((n_node,))],
+        compiler_params=pltpu.CompilerParams(
+            collective_id=0, has_side_effects=True, vmem_limit_bytes=32 * 1024 * 1024
+        ),
+    )(same, x_rows, x_trans, counts, degrees, w_self, w_neigh, out_bias.reshape(1, hid), d_out)
+    steps = 8
+    grad_cols = pl.pallas_call(
+        place_kernel,
+        grid=(steps,),
+        out_shape=jax.ShapeDtypeStruct(features.shape, BF16),
+        in_specs=[smem, vmem, vmem],
+        out_specs=pl.BlockSpec((rows, src_width // steps), lambda i: (0, i)),
+        compiler_params=pltpu.CompilerParams(vmem_limit_bytes=16 * 1024 * 1024),
+    )(position, spread, back_self)
+    return (output, grad_cols, grad_neigh)
+
+
+def fits_kernel(n_node, n_feat):
+    return n_feat == 4 and n_node == 8
+
 
 def solution(mesh):
+    n_node, n_feat = mesh.shape["node"], mesh.shape["feat"]
     placed = (
         P("feat", "node"),
         P("node", None),
@@ -94,7 +435,7 @@
         P(("node", "feat"), None),
     )
     return jax.shard_map(
-        body,
+        functools.partial(kernel_body, n_node) if fits_kernel(n_node, n_feat) else body,
         mesh=mesh,
         in_specs=placed,
         out_specs=(P(("node", "feat"), None), P("feat", "node"), P("feat", "node")),

time: 172 us -> 44.9 us (0.26)
  waiting for transfers between devices: 90.4 us -> 0 us
  Pallas kernels: 0 us -> 36.9 us
  other arithmetic: 20.6 us -> 0.17 us
  starting transfers between devices: 14.5 us -> 0 us
  between operations: 13.9 us -> 0.73 us
  local copies, waits for them, and re-layouts: 19.6 us -> 6.9 us
  matrix products: 12.4 us -> 0 us
    reduce_scatter x2 -> x0, waiting for transfers between devices: 67 us -> none  [the longest x1 53.6 us: body(): lax.psum_scatter(reduced, 'node', scatter_dimension=1, tiled=True)]
    pallas_call x0 -> x3, Pallas kernels: none -> 36.9 us  [the longest x1 28.3 us: kernel_body(): pl.pallas_call(functools.partial(layer_kernel, n_node, 1.0 / math.sqrt(no...]
    all_gather x2 -> x0, waiting for transfers between devices: 14.6 us -> none  [the longest x1 14.6 us: body(): lax.all_gather(w_neigh, 'feat', axis=0, tiled=True)]
    all_to_all x4 -> x0, starting transfers between devices: 14.3 us -> none  [the longest x1 4.24 us: body(): lax.all_to_all(own_cols, 'feat', split_axis=1, concat_axis=0, tiled=True)]
    dot_general x7 -> x0, matrix products: 12.4 us -> none  [the longest x2 4.71 us: dot_rows(): lax.dot_general(left_cols, weights, (((0,), (0,)), ((), ())), preferred_e...]
    reshape x3 -> x2, local copies, waits for them, and re-layouts: 9.58 us -> 0.87 us  [kernel_body(): nbrs = neighbors.reshape(blocks, BLOCK, -1).transpose(0, 2, 1)]
    all_to_all x4 -> x0, waiting for transfers between devices: 7.26 us -> none  [the longest x1 3.82 us: body(): lax.all_to_all(back_neigh, 'feat', split_axis=0, concat_axis=1, tiled=True)]
    scatter-add x2 -> x0, other arithmetic: 6.52 us -> none  [the longest x1 3.99 us: body(): jax.ops.segment_sum(by_block, tile_src.reshape(-1), num_segments=src_widt...]
  transfers between devices with their start and end apart: 8 -> 0, of which waited for: 5 -> 0; matrix products, arithmetic and copies ran while one was open for 28% -> 0% of each run, Pallas kernels for 0% -> 0%
where the time goes in v1:
time: 44.9 us; the launch traced here: 44.7 us
  Pallas kernels  36.9 us (82%)
  local copies, waits for them, and re-layouts  6.9 us (15%)
  between operations  0.73 us (2%)
    pallas_call x1, Pallas kernels, kernel_body(): pl.pallas_call(functools.partial(layer_kernel, n_node, 1.0 / math.sqrt(no...  28.3 us
    unnamed x20, local copies, waits for them, and re-layouts  5.27 us
    pallas_call x1, Pallas kernels, kernel_body(): pl.pallas_call(gather_kernel, out_shape=(jax.ShapeDtypeStruct((2 * rows,...  4.44 us
    pallas_call x1, Pallas kernels, kernel_body(): pl.pallas_call(place_kernel, grid=(steps,), out_shape=jax.ShapeDtypeStruc...  4.16 us

profile of v1, /device:TPU:0, one launch (start us, length us, event | category | flops | bytes accessed | tf_op | source)
XLA Modules:
  0.0 44.7 jit_solution(3836038934740327287)
XLA Ops:
  0.6 0.0 copy-start.7
  0.6 0.0 copy-start.6
  0.7 0.8 %eq.28 = s32[16]{0:T(128)S(1)} reshape(s32[4,4]{1,0:T(4,128)} %tile_src.1) | data formatting | bytes 128 | tf_op jit(solution)/shard_map/eq | solution.py:358
  1.4 0.1 select_reduce_fusion
  1.5 0.1 compare_convert_fusion.same
  1.6 0.9 %reshape.17 = s32[4,128,25]{1,0,2:T(4,128)S(1)} reshape(s32[512,25]{0,1:T(8,128)} %param.10) | data formatting | bytes 102400 | tf_op jit(solution)/shard_map/reshape | solution.py:357
  2.5 0.0 copy-start
  2.5 1.9 %copy-done = bf16[192,8192]{1,0:T(8,128)(2,1)S(1)} copy-done((bf16[192,8192]{1,0:T(8,128)(2,1)S(1)}, bf16[192,8192]{1,0:T(8,128)(2,1)}, u32[]{:S(2)}) %copy-start) | copy-done | bytes 3145752
  4.4 0.0 copy-start.4
  4.4 0.7 %copy-done.4 = s32[4,4]{1,0:T(4,128)S(1)} copy-done((s32[4,4]{1,0:T(4,128)S(1)}, s32[4,4]{1,0:T(4,128)}, u32[]{:S(2)}) %copy-start.4) | copy-done | bytes 88
  5.0 0.0 copy-start.5
  5.1 0.7 %copy-done.5 = s32[512]{0:T(512)S(1)} copy-done((s32[512]{0:T(512)S(1)}, s32[512]{0:T(512)}, u32[]{:S(2)}) %copy-start.5) | copy-done | bytes 2072
  5.7 0.0 copy-start.8
  5.7 0.7 %copy-done.8 = s32[4]{0:T(128)S(1)} copy-done((s32[4]{0:T(128)S(1)}, s32[4]{0:T(128)}, u32[]{:S(2)}) %copy-start.8) | copy-done | bytes 40
  6.4 0.0 copy-start.1
  6.4 0.0 copy-start.2
  6.4 0.0 copy-start.3
  6.4 4.4 %shard_map.112 = (bf16[384,512]{1,0:T(8,128)(2,1)S(1)}, bf16[512,384]{1,0:T(8,128)(2,1)S(1)}, bf16[16,128,128]{2,1,0:T(8,128)(2,1)S(1)}) custom-call(s32[4,4]{1,0:T(4,128)S(1)} %copy-done.4, s32[4]{0:T(128)S(1)} %copy-done.8, bf16[192,8192]{1,0:T(8,128)(2,1)S(1)} %copy-done, s32[4,25,128]{2,1,0:T(8,128)S(1)} %bitcast.7, s32[4,1,128]{2,1,0:T(1,128)S(1)} %bitcast.8), custom_call_target="tpu_custom_call" | custom-call | tf_op jit(solution)/shard_map/pallas_call | solution.py:363
  10.8 0.0 copy-done.7
  10.8 0.0 copy-done.6
  10.9 0.0 copy-done.1
  10.9 0.0 copy-done.2
  10.9 0.0 copy-done.3
  10.9 28.3 %shard_map.113 = (bf16[128,1024]{1,0:T(8,128)(2,1)S(1)}, f32[16,192,128]{2,1,0:T(8,128)S(1)}, bf16[192,512]{1,0:T(8,128)(2,1)S(1)}, f32[192,128]{1,0:T(8,128)S(1)}) custom-call(f32[16,16]{1,0:T(8,128)S(1)} %compare_convert_fusion.same, bf16[384,512]{1,0:T(8,128)(2,1)S(1)} %get-tuple-element.10.x_rows, bf16[512,384]{1,0:T(8,128)(2,1)S(1)} %get-tuple-element.11.x_trans, ...), custom_call_target="tpu_custom_call" | custom-call | tf_op jit(solution)/shard_map/pallas_call | solution.py:380
  39.2 4.2 %shard_map.114 = bf16[192,8192]{1,0:T(8,128)(2,1)} custom-call(s32[64]{0:T(128)S(1)} %compare_select_fusion.position, f32[16,192,128]{2,1,0:T(8,128)S(1)} %get-tuple-element.14.spread, bf16[192,512]{1,0:T(8,128)(2,1)S(1)} %get-tuple-element.15.back_self), custom_call_target="tpu_custom_call" | custom-call | tf_op jit(solution)/shard_map/pallas_call | solution.py:409
  43.3 0.7 %copy.18 = bf16[128,1024]{1,0:T(8,128)(2,1)} copy(bf16[128,1024]{1,0:T(8,128)(2,1)S(1)} %get-tuple-element.20) | data formatting | bytes 524288
  44.0 0.6 %copy.19 = f32[192,128]{1,0:T(8,128)} copy(f32[192,128]{1,0:T(8,128)S(1)} %get-tuple-element.22) | data formatting | bytes 196608
  (2 shorter events, 0.0 us)
Async XLA Ops:
  0.6 10.2 %copy-start.7 = (f32[1024]{0:T(1024)S(1)}, f32[1024]{0:T(1024)}, u32[]{:S(2)}) copy-start(f32[1024]{0:T(1024)} %param.16) | copy-start | bytes 12292
  0.6 10.2 %copy-start.6 = (s32[512]{0:T(512)S(1)}, s32[512]{0:T(512)}, u32[]{:S(2)}) copy-start(s32[512]{0:T(512)} %param.11) | copy-start | bytes 6148
  2.5 1.9 %copy-start = (bf16[192,8192]{1,0:T(8,128)(2,1)S(1)}, bf16[192,8192]{1,0:T(8,128)(2,1)}, u32[]{:S(2)}) copy-start(bf16[192,8192]{1,0:T(8,128)(2,1)} %features.1) | copy-start | bytes 9437188
  4.4 0.7 %copy-start.4 = (s32[4,4]{1,0:T(4,128)S(1)}, s32[4,4]{1,0:T(4,128)}, u32[]{:S(2)}) copy-start(s32[4,4]{1,0:T(4,128)} %tile_src.1) | copy-start | bytes 196
  5.0 0.7 %copy-start.5 = (s32[512]{0:T(512)S(1)}, s32[512]{0:T(512)}, u32[]{:S(2)}) copy-start(s32[512]{0:T(512)} %param.11) | copy-start | bytes 6148
  5.7 0.7 %copy-start.8 = (s32[4]{0:T(128)S(1)}, s32[4]{0:T(128)}, u32[]{:S(2)}) copy-start(s32[4]{0:T(128)} %tile_count.1) | copy-start | bytes 52
  6.4 4.5 %copy-start.1 = (bf16[192,1024]{1,0:T(8,128)(2,1)S(1)}, bf16[192,1024]{1,0:T(8,128)(2,1)}, u32[]{:S(2)}) copy-start(bf16[192,1024]{1,0:T(8,128)(2,1)} %w_self.1) | copy-start | bytes 1179652
  6.4 4.5 %copy-start.2 = (bf16[192,1024]{1,0:T(8,128)(2,1)S(1)}, bf16[192,1024]{1,0:T(8,128)(2,1)}, u32[]{:S(2)}) copy-start(bf16[192,1024]{1,0:T(8,128)(2,1)} %w_neigh.1) | copy-start | bytes 1179652
  6.4 4.5 %copy-start.3 = (bf16[128,1024]{1,0:T(8,128)(2,1)S(1)}, bf16[128,1024]{1,0:T(8,128)(2,1)}, u32[]{:S(2)}) copy-start(bf16[128,1024]{1,0:T(8,128)(2,1)} %d_out.1) | copy-start | bytes 786436
